TPU v7x, 32 devices: a whole 2x2x4 slice. The times are simulated.
32 devices in a mesh: dp: 32 (over z, y, x, core).
Axes of the slice: x: 2, y: 2, z: 4, core: 2. Of those that a mesh axis runs over, the one named last changes fastest.
Arguments:
- tokens: bfloat16 [64, 512, 512], P('dp'), may hold values from -6 to 6
- memory: bfloat16 [64, 512, 512], P('dp'), may hold values from -6 to 6
- segments: int32 [64, 512], P('dp'), may hold values from 0 to 3, never falling along the last dimension, each value on 1 to 256 neighbouring positions
- cotangent: bfloat16 [64, 512, 512], P('dp'), may hold values from -6 to 6
- group_sizes: int32 [8], replicated, may hold values from 1 to 8, 32 in all
- task_embed: bfloat16 [8, 64], replicated, may hold values from -4 to 4
- position_embed: bfloat16 [2, 64], replicated, may hold values from -4 to 4
- hyper_first: bfloat16 [64, 128], replicated, may hold values from -0.75 to 0.75
- hyper_second: bfloat16 [128, 64], replicated, may hold values from -0.5 to 0.5
- hyper_gain: bfloat16 [64, 1536], replicated, may hold values from -0.375 to 0.375
- hyper_down: bfloat16 [64, 8192], replicated, may hold values from -0.03125 to 0.03125
- hyper_up: bfloat16 [64, 8192], replicated, may hold values from -0.1875 to 0.1875
- self_qkv: bfloat16 [3, 512, 512], replicated, may hold values from -0.25 to 0.25
- self_out: bfloat16 [512, 512], replicated, may hold values from -0.75 to 0.75
- cross_qkv: bfloat16 [3, 512, 512], replicated, may hold values from -0.25 to 0.25
- cross_out: bfloat16 [512, 512], replicated, may hold values from -1.5 to 1.5
- ffn_in: bfloat16 [512, 2048], replicated, may hold values from -0.25 to 0.25
- ffn_out: bfloat16 [2048, 512], replicated, may hold values from -0.125 to 0.125
Outputs:
- output: bfloat16 [64, 512, 512], P('dp')
- input_grad: float32 [64, 512, 512], P('dp')
- memory_grad: float32 [64, 512, 512], P('dp')
- task_grad: float32 [8, 64], replicated
- position_grad: float32 [2, 64], replicated
- hyper_first_grad: float32 [64, 128], replicated
- hyper_second_grad: float32 [128, 64], replicated
- hyper_gain_grad: float32 [64, 1536], replicated
- hyper_down_grad: float32 [64, 8192], replicated
- hyper_up_grad: float32 [64, 8192], replicated
- self_qkv_grad: float32 [3, 512, 512], replicated
- self_out_grad: float32 [512, 512], replicated
- cross_qkv_grad: float32 [3, 512, 512], replicated
- cross_out_grad: float32 [512, 512], replicated
- ffn_in_grad: float32 [512, 2048], replicated
- ffn_out_grad: float32 [2048, 512], replicated
Inputs may be any that keep to these rules, and one draw needn't show every extreme that they name: The devices of dp belong to tasks in order: the first group_sizes[0] devices to task 0, the next group_sizes[1] to task 1, and so on; the sizes add up to 32. `segments`: along each row the segment numbers never fall; every segment holds at most 256 positions.
All inputs are finite; a program needn't handle non-finite values.
Results may differ from a plain program's by a relative error of at most 0.024.
Values sent between devices are 32-bit elements; how exact they have to be, the bound alone decides.
No kernel may reach another device: no remote copies, remote signals or barrier semaphores. Data moves between devices by JAX's collectives and lax.ppermute only.
A program may use at most 192 MiB of HBM per device.

v0:
```python
import jax
import jax.numpy as jnp
from jax import lax
from jax.sharding import PartitionSpec as P

HEADS = 8
HEAD_DIM = 64


epsilon = 1e-06
highest = lax.Precision.HIGHEST


def rms_scale(values, gain_vec):
    return (
        values * lax.rsqrt(jnp.mean(values * values, axis=-1, keepdims=True) + epsilon) * gain_vec
    )


def matmul(left, right):
    return jnp.dot(left, right, preferred_element_type=jnp.float32)


def left_matmul(left, right):
    return lax.dot_general(
        left, right, (((0,), (0,)), ((), ())), preferred_element_type=jnp.float32
    )


def right_matmul(left, right):
    return lax.dot_general(
        left, right, (((1,), (1,)), ((), ())), preferred_element_type=jnp.float32
    )


def split_heads(values):
    return values.reshape(values.shape[0], values.shape[1], HEADS, HEAD_DIM)


def head_scores(head_q, head_k, allowed, masked):
    scores = jnp.einsum(
        "bqhd,bkhd->bhqk", head_q, head_k, preferred_element_type=jnp.float32
    ) * HEAD_DIM ** (-0.5)
    if masked:
        scores = jnp.where(allowed[:, None], scores, -1000000000.0)
    return scores


def attend(queries, key_rows, value_rows, allowed, masked):
    scores = head_scores(split_heads(queries), split_heads(key_rows), allowed, masked)
    top_score = jnp.max(scores, axis=-1, keepdims=True)
    expo = jnp.exp(scores - top_score)
    totals = jnp.sum(expo, axis=-1, keepdims=True)
    probs = (expo / totals).astype(jnp.bfloat16)
    mixed = jnp.einsum(
        "bhqk,bkhd->bqhd", probs, split_heads(value_rows), preferred_element_type=jnp.float32
    )
    return (mixed.reshape(queries.shape).astype(jnp.bfloat16), top_score + jnp.log(totals))


def attend_back(queries, key_rows, value_rows, allowed, masked, logsum, grad_mixed):
    head_q = split_heads(queries)
    head_k = split_heads(key_rows)
    head_v = split_heads(value_rows)
    head_g = split_heads(grad_mixed)
    probs = jnp.exp(head_scores(head_q, head_k, allowed, masked) - logsum)
    grad_probs = jnp.einsum("bqhd,bkhd->bhqk", head_g, head_v, preferred_element_type=jnp.float32)
    grad_values = jnp.einsum(
        "bhqk,bqhd->bkhd", probs.astype(jnp.bfloat16), head_g, preferred_element_type=jnp.float32
    )
    delta = jnp.sum(probs * grad_probs, axis=-1, keepdims=True)
    grad_scores = (probs * (grad_probs - delta)).astype(jnp.bfloat16)
    scale_now = HEAD_DIM ** (-0.5)
    grad_queries = (
        jnp.einsum("bhqk,bkhd->bqhd", grad_scores, head_k, preferred_element_type=jnp.float32)
        * scale_now
    )
    grad_keys = (
        jnp.einsum("bhqk,bqhd->bkhd", grad_scores, head_q, preferred_element_type=jnp.float32)
        * scale_now
    )
    return (
        grad_queries.reshape(queries.shape).astype(jnp.bfloat16),
        grad_keys.reshape(key_rows.shape).astype(jnp.bfloat16),
        grad_values.reshape(value_rows.shape).astype(jnp.bfloat16),
    )


def silu_back(values, grad_out):
    return jax.vjp(jax.nn.silu, values)[1](grad_out)[0]


def on_device(
    tokens,
    memory,
    segments,
    cotangent,
    group_sizes,
    task_embed,
    position_embed,
    hyper_first,
    hyper_second,
    hyper_gain,
    hyper_down,
    hyper_up,
    self_qkv,
    self_out,
    cross_qkv,
    cross_out,
    ffn_in,
    ffn_out,
):
    row_count, seq_len, model_width = tokens.shape
    mem_len = memory.shape[1]
    token_count = row_count * seq_len
    devices = lax.axis_size("dp")
    place = lax.axis_index("dp")
    ntask = group_sizes.shape[0]
    emb_width = task_embed.shape[1]
    ends = jnp.cumsum(group_sizes)
    task_now = jnp.sum((ends <= place).astype(jnp.int32))
    onehot = (jnp.arange(ntask) == task_now).astype(jnp.float32)
    share = devices / (ntask * jnp.sum(onehot * group_sizes.astype(jnp.float32)))
    table = task_embed.astype(jnp.float32)
    first_f = hyper_first.astype(jnp.float32)
    second_f = hyper_second.astype(jnp.float32)
    gain_f = hyper_gain.astype(jnp.float32)
    down_f = hyper_down.astype(jnp.float32)
    up_f = hyper_up.astype(jnp.float32)
    position_f = position_embed.astype(jnp.float32)
    embed = jnp.dot(onehot, table, precision=highest)
    pre_act = jnp.dot(embed, first_f, precision=highest)
    hidden = jax.nn.silu(pre_act)
    code = jnp.dot(hidden, second_f, precision=highest)
    gains = 1.0 + jnp.dot(code, gain_f, precision=highest).reshape(3, model_width)
    codes = code[None, :] + position_f
    down_w = (
        jnp.dot(codes, down_f, precision=highest).reshape(2, model_width, -1).astype(jnp.bfloat16)
    )
    up_w = jnp.dot(codes, up_f, precision=highest).reshape(2, -1, model_width).astype(jnp.bfloat16)
    flat_x = tokens.reshape(token_count, model_width).astype(jnp.float32)
    mem_flat = memory.reshape(row_count * mem_len, model_width)
    positions = jnp.arange(seq_len)
    allowed = (segments[:, :, None] == segments[:, None, :]) & (
        positions[:, None] >= positions[None, :]
    )[None]
    row_shape = (row_count, seq_len, model_width)
    mem_shape = (row_count, mem_len, model_width)
    in_one = rms_scale(flat_x, gains[0]).astype(jnp.bfloat16)
    self_parts = jnp.einsum(
        "nd,jde->jne", in_one, self_qkv, preferred_element_type=jnp.float32
    ).astype(jnp.bfloat16)
    self_q = self_parts[0].reshape(row_shape)
    self_k = self_parts[1].reshape(row_shape)
    self_v = self_parts[2].reshape(row_shape)
    mixed_one, logsum_one = attend(self_q, self_k, self_v, allowed, True)
    mixed_one = mixed_one.reshape(token_count, model_width)
    branch = matmul(mixed_one, self_out)
    branch_low = branch.astype(jnp.bfloat16)
    narrow = matmul(branch_low, down_w[0])
    narrow_act = jax.nn.silu(narrow).astype(jnp.bfloat16)
    after_one = flat_x + branch + matmul(narrow_act, up_w[0])
    in_two = rms_scale(after_one, gains[1]).astype(jnp.bfloat16)
    query_two = matmul(in_two, cross_qkv[0]).astype(jnp.bfloat16).reshape(row_shape)
    mem_parts = jnp.einsum(
        "nd,jde->jne", mem_flat, cross_qkv[1:], preferred_element_type=jnp.float32
    ).astype(jnp.bfloat16)
    key_two = mem_parts[0].reshape(mem_shape)
    value_two = mem_parts[1].reshape(mem_shape)
    mixed_two, logsum_two = attend(query_two, key_two, value_two, allowed, False)
    mixed_two = mixed_two.reshape(token_count, model_width)
    after_two = after_one + matmul(mixed_two, cross_out)
    in_three = rms_scale(after_two, gains[2]).astype(jnp.bfloat16)
    inner = matmul(in_three, ffn_in)
    inner_act = jax.nn.gelu(inner, approximate=False).astype(jnp.bfloat16)
    outer = matmul(inner_act, ffn_out)
    outer_low = outer.astype(jnp.bfloat16)
    narrow_two = matmul(outer_low, down_w[1])
    narrow_two_act = jax.nn.silu(narrow_two).astype(jnp.bfloat16)
    result = after_two + outer + matmul(narrow_two_act, up_w[1])
    output = result.astype(jnp.bfloat16).reshape(row_shape)
    grad_now = cotangent.reshape(token_count, model_width).astype(jnp.float32) * share
    grad_low = grad_now.astype(jnp.bfloat16)
    up_grad_two = left_matmul(narrow_two_act, grad_low)
    d_narrow_two = silu_back(narrow_two, right_matmul(grad_low, up_w[1])).astype(jnp.bfloat16)
    down_grad_two = left_matmul(outer_low, d_narrow_two)
    d_outer = (grad_now + right_matmul(d_narrow_two, down_w[1])).astype(jnp.bfloat16)
    ffn_out_grad = left_matmul(inner_act, d_outer)
    gelu_pull = jax.vjp(lambda values: jax.nn.gelu(values, approximate=False), inner)[1]
    d_inner = gelu_pull(right_matmul(d_outer, ffn_out))[0].astype(jnp.bfloat16)
    ffn_in_grad = left_matmul(in_three, d_inner)
    norm_pull = jax.vjp(rms_scale, after_two, gains[2])[1]
    d_after, gain_grad_three = norm_pull(right_matmul(d_inner, ffn_in))
    grad_now = grad_now + d_after
    grad_low = grad_now.astype(jnp.bfloat16)
    cross_out_grad = left_matmul(mixed_two, grad_low)
    d_mixed_two = right_matmul(grad_low, cross_out).astype(jnp.bfloat16).reshape(row_shape)
    d_query_two, d_key_two, d_value_two = attend_back(
        query_two, key_two, value_two, allowed, False, logsum_two, d_mixed_two
    )
    d_query_two = d_query_two.reshape(token_count, model_width)
    d_key_two = d_key_two.reshape(row_count * mem_len, model_width)
    d_value_two = d_value_two.reshape(row_count * mem_len, model_width)
    cross_qkv_grad = jnp.stack(
        [
            left_matmul(in_two, d_query_two),
            left_matmul(mem_flat, d_key_two),
            left_matmul(mem_flat, d_value_two),
        ]
    )
    memory_grad = right_matmul(d_key_two, cross_qkv[1]) + right_matmul(d_value_two, cross_qkv[2])
    norm_pull = jax.vjp(rms_scale, after_one, gains[1])[1]
    d_after, gain_grad_two = norm_pull(right_matmul(d_query_two, cross_qkv[0]))
    grad_now = grad_now + d_after
    grad_low = grad_now.astype(jnp.bfloat16)
    up_grad_one = left_matmul(narrow_act, grad_low)
    d_narrow = silu_back(narrow, right_matmul(grad_low, up_w[0])).astype(jnp.bfloat16)
    down_grad_one = left_matmul(branch_low, d_narrow)
    d_branch = (grad_now + right_matmul(d_narrow, down_w[0])).astype(jnp.bfloat16)
    self_out_grad = left_matmul(mixed_one, d_branch)
    d_mixed_one = right_matmul(d_branch, self_out).astype(jnp.bfloat16).reshape(row_shape)
    d_self = attend_back(self_q, self_k, self_v, allowed, True, logsum_one, d_mixed_one)
    d_stack = jnp.stack([part.reshape(token_count, model_width) for part in d_self])
    self_qkv_grad = jnp.einsum("nd,jne->jde", in_one, d_stack, preferred_element_type=jnp.float32)
    d_in_one = jnp.einsum("jne,jde->nd", d_stack, self_qkv, preferred_element_type=jnp.float32)
    norm_pull = jax.vjp(rms_scale, flat_x, gains[0])[1]
    d_x, gain_grad_one = norm_pull(d_in_one)
    input_grad = (grad_now + d_x).reshape(row_shape)
    down_grads = jnp.stack([down_grad_one.reshape(-1), down_grad_two.reshape(-1)])
    up_grads = jnp.stack([up_grad_one.reshape(-1), up_grad_two.reshape(-1)])
    gain_grads = jnp.concatenate([gain_grad_one, gain_grad_two, gain_grad_three])
    extra_down = jnp.dot(codes.T, down_grads, precision=highest).reshape(-1)
    extra_up = jnp.dot(codes.T, up_grads, precision=highest).reshape(-1)
    extra_gain = jnp.outer(code, gain_grads).reshape(-1)
    d_codes = jnp.dot(down_grads, down_f.T, precision=highest) + jnp.dot(
        up_grads, up_f.T, precision=highest
    )
    d_code = jnp.sum(d_codes, axis=0) + jnp.dot(gain_f, gain_grads, precision=highest)
    own_second = jnp.outer(hidden, d_code)
    d_pre = silu_back(pre_act, jnp.dot(second_f, d_code, precision=highest))
    own_first = jnp.outer(embed, d_pre)
    own_task = jnp.outer(onehot, jnp.dot(first_f, d_pre, precision=highest))
    small = lax.psum((own_first, own_second, d_codes, own_task), "dp")
    shares = (
        lax.psum_scatter(self_qkv_grad.reshape(-1), "dp", scatter_dimension=0, tiled=True),
        lax.psum_scatter(self_out_grad.reshape(-1), "dp", scatter_dimension=0, tiled=True),
        lax.psum_scatter(cross_qkv_grad.reshape(-1), "dp", scatter_dimension=0, tiled=True),
        lax.psum_scatter(cross_out_grad.reshape(-1), "dp", scatter_dimension=0, tiled=True),
        lax.psum_scatter(ffn_in_grad.reshape(-1), "dp", scatter_dimension=0, tiled=True),
        lax.psum_scatter(ffn_out_grad.reshape(-1), "dp", scatter_dimension=0, tiled=True),
        lax.psum_scatter(extra_down, "dp", scatter_dimension=0, tiled=True),
        lax.psum_scatter(extra_up, "dp", scatter_dimension=0, tiled=True),
        lax.psum_scatter(extra_gain, "dp", scatter_dimension=0, tiled=True),
    )
    whole = (
        lax.all_gather(shares[0], "dp", axis=0, tiled=True),
        lax.all_gather(shares[1], "dp", axis=0, tiled=True),
        lax.all_gather(shares[2], "dp", axis=0, tiled=True),
        lax.all_gather(shares[3], "dp", axis=0, tiled=True),
        lax.all_gather(shares[4], "dp", axis=0, tiled=True),
        lax.all_gather(shares[5], "dp", axis=0, tiled=True),
        lax.all_gather(shares[6], "dp", axis=0, tiled=True),
        lax.all_gather(shares[7], "dp", axis=0, tiled=True),
        lax.all_gather(shares[8], "dp", axis=0, tiled=True),
    )
    hyper_down_grad = whole[6].reshape(emb_width, -1)
    hyper_up_grad = whole[7].reshape(emb_width, -1)
    hyper_gain_grad = whole[8].reshape(emb_width, -1)
    hyper_first_grad, hyper_second_grad, position_grad, task_grad = small
    return (
        output,
        input_grad,
        memory_grad.reshape(mem_shape),
        task_grad,
        position_grad,
        hyper_first_grad,
        hyper_second_grad,
        hyper_gain_grad,
        hyper_down_grad,
        hyper_up_grad,
        whole[0].reshape(self_qkv.shape),
        whole[1].reshape(self_out.shape),
        whole[2].reshape(cross_qkv.shape),
        whole[3].reshape(cross_out.shape),
        whole[4].reshape(ffn_in.shape),
        whole[5].reshape(ffn_out.shape),
    )


def solution(mesh):
    placed = (
        P("dp", None, None),
        P("dp", None, None),
        P("dp", None),
        P("dp", None, None),
        P(),
        P(),
        P(),
        P(),
        P(),
        P(),
        P(),
        P(),
        P(),
        P(),
        P(),
        P(),
        P(),
        P(),
    )
    return jax.shard_map(
        on_device,
        mesh=mesh,
        in_specs=placed,
        out_specs=(
            P("dp", None, None),
            P("dp", None, None),
            P("dp", None, None),
            P(),
            P(),
            P(),
            P(),
            P(),
            P(),
            P(),
            P(),
            P(),
            P(),
            P(),
            P(),
            P(),
        ),
        check_vma=False,
    )
```

profile of v0, /device:TPU:0, one launch (start us, length us, event | category | flops | bytes accessed | tf_op | source)
XLA Modules:
  0.0 1322.5 jit_solution(6859871586716510527)
XLA Ops:
  64.5 10.1 fusion.121
  74.6 8.4 fusion
  83.6 7.5 fusion.43
  106.2 8.3 multiply_reduce_fusion.2
  114.4 8.7 fusion.1
  123.2 7.7 fusion.44
  133.9 21.8 %multiply_convert_fusion.2 = (bf16[1024,2048]{1,0:T(8,128)(2,1)S(1)}, f32[1024,2048]{1,0:T(8,128)S(1)}, f32[1024,2048]{1,0:T(8,128)}) fusion(bf16[512,2048]{1,0:T(8,128)(2,1)S(1)} %copy-done, f32[1024,512]{1,0:T(8,128)S(1)} %get-tuple-element.58, f32[512]{0:T(512)S(1)} %get-tuple-element.48, f32[1024]{0:T(1024)S(1)} %fusion.88), kind=kOutput, calls=%fused_computation.25 | convolution fusion | flops 2285371392 | bytes 25171968 | tf_op jit(solution)/shard_map/dot_general | solution.py:21
  161.0 4.4 convolution_bitcast_fusion
  165.4 7.3 add_convert_fusion
  175.3 4.5 convolution_bitcast_fusion.1
  190.1 8.6 fusion.34
  198.7 11.3 multiply_reduce_fusion.1
  210.1 12.1 multiply_convert_fusion.1
  244.7 9.5 fusion.40
  254.2 11.3 multiply_reduce_fusion
  265.5 11.8 multiply_convert_fusion
  306.3 5.5 copy.207
  333.6 4.4 copy.202
  339.0 367.3 %all-reduce.16.cloned.1.call-done = (f32[98304]{0:T(1024)}, f32[524288]{0:T(1024)}, f32[524288]{0:T(1024)}, f32[786432]{0:T(1024)}, f32[262144]{0:T(1024)}, /*in...) async-done(((f32[98304]{0:T(1024)}, f32[524288]{0:T(1024)}, f32[524288]{0:T(1024)}, f32[786432]{0:T(1024)}, f32[262144]{0:T(1024)}, ...) | async-done | bytes 21364752
  743.9 40.7 %all_gather.27 = f32[98304]{0:T(1024)S(1)} all-gather(f32[3072]{0:T(1024)S(1)} %dynamic-slice), channel_id=1, replica_groups=mesh['dp'=32] {'dp'}, dimensions={0}, use_global_device_ids=true | all-gather | bytes 405504 | tf_op jit(solution)/shard_map/all_gather | solution.py:264
  787.7 31.1 %all-gather.15.cloned.1.call-done = f32[262144]{0:T(1024)} async-done(((f32[8192]{0:T(1024)}), f32[262144]{0:T(1024)}) %all-gather.15.cloned.1.call-update) | async-done | bytes 1048592 | tf_op jit(solution)/shard_map/all_gather | solution.py:257
  821.2 55.7 %all-gather.11.cloned.1.call-done = f32[524288]{0:T(1024)} async-done(((f32[16384]{0:T(1024)}), f32[524288]{0:T(1024)}) %all-gather.11.cloned.1.call-update) | async-done | bytes 2097168 | tf_op jit(solution)/shard_map/all_gather | solution.py:263
  879.7 55.2 %all-gather.9.cloned.1.call-done = f32[524288]{0:T(1024)} async-done(((f32[16384]{0:T(1024)}), f32[524288]{0:T(1024)}) %all-gather.9.cloned.1.call-update) | async-done | bytes 2097168 | tf_op jit(solution)/shard_map/all_gather | solution.py:262
  937.6 58.4 %all-gather.17.cloned.1.call-done = f32[786432]{0:T(1024)} async-done(((f32[24576]{0:T(1024)}), f32[786432]{0:T(1024)}) %all-gather.17.cloned.1.call-update) | async-done | bytes 3145744 | tf_op jit(solution)/shard_map/all_gather | solution.py:258
  996.0 4.6 reshape.345
  1000.6 56.7 %all-gather.13.cloned.1.call-done = f32[786432]{0:T(1024)} async-done(((f32[24576]{0:T(1024)}), f32[786432]{0:T(1024)}) %all-gather.13.cloned.1.call-update) | async-done | bytes 3145744 | tf_op jit(solution)/shard_map/all_gather | solution.py:256
  1057.3 4.6 reshape.341
  1061.8 59.8 %all-gather.23.cloned.1.call-done = f32[1048576]{0:T(1024)} async-done(((f32[32768]{0:T(1024)}), f32[1048576]{0:T(1024)}) %all-gather.23.cloned.1.call-update) | async-done | bytes 4194320 | tf_op jit(solution)/shard_map/all_gather | solution.py:261
  1121.6 5.1 reshape.351
  1126.6 59.0 %all-gather.21.cloned.1.call-done = f32[1048576]{0:T(1024)} async-done(((f32[32768]{0:T(1024)}), f32[1048576]{0:T(1024)}) %all-gather.21.cloned.1.call-update) | async-done | bytes 4194320 | tf_op jit(solution)/shard_map/all_gather | solution.py:260
  1185.6 4.9 reshape.349
  1190.5 119.7 %all-reduce.14.cloned.1.call-done = (f32[8,64]{1,0:T(8,128)}, f32[2,64]{1,0:T(2,128)}, f32[64,128]{1,0:T(8,128)}, f32[128,64]{0,1:T(8,128)}) async-done(((f32[8,64]{1,0:T(8,128)}, f32[2,64]{1,0:T(2,128)}, f32[64,128]{1,0:T(8,128)}, f32[128,64]{0,1:T(8,128)}), (f32[8,64]{1,0:T(8,128)}, f32[2,64]{1,0:T(2,128)}, f32[64,128]{1,0:T(8,128)}, f32[128,64]{0,1:T(8,128)})) %all-reduce.14.cloned.1.call-update) | async-done | bytes 68112 | tf_op jit(solution)/shard_map/psum | solution.py:243
  (344 shorter events, 220.4 us)
Async XLA Ops:
  7.2 126.8 %copy-start = (bf16[512,2048]{1,0:T(8,128)(2,1)S(1)}, bf16[512,2048]{1,0:T(8,128)(2,1)}, u32[]{:S(2)}) copy-start(bf16[512,2048]{1,0:T(8,128)(2,1)} %param.34) | copy-start | bytes 6291460
  7.2 699.0 %all-reduce.16.cloned.1.call-start = ((), (), s32[]{:S(2)}) async-start(), calls=%async_computation.9 | async-start | bytes 42729472
  14.4 21.8 %copy-start.64 = (f32[1024]{0:T(1024)}, f32[1024]{0:T(1024)S(1)}, u32[]{:S(2)}) copy-start(f32[1024]{0:T(1024)S(1)} %rsqrt.33) | copy-start | bytes 12292
  16.7 8.4 copy-start.74
  17.9 18.3 %copy-start.71 = (f32[512]{0:T(512)}, f32[512]{0:T(512)S(1)}, u32[]{:S(2)}) copy-start(f32[512]{0:T(512)S(1)} %get-tuple-element.50) | copy-start | bytes 6148
  17.9 76.7 %copy-start.62 = (f32[512]{0:T(512)}, f32[512]{0:T(512)S(1)}, u32[]{:S(2)}) copy-start(f32[512]{0:T(512)S(1)} %get-tuple-element.49) | copy-start | bytes 6148
  19.9 113.5 %copy-start.54 = (bf16[16,512]{1,0:T(8,128)(2,1)}, bf16[16,512]{1,0:T(8,128)(2,1)S(1)}, u32[]{:S(2)}) copy-start(bf16[16,512]{1,0:T(8,128)(2,1)S(1)} %squeeze.30) | copy-start | bytes 49156
  19.9 73.7 %copy-start.56 = (bf16[16,512]{1,0:T(8,128)(2,1)}, bf16[16,512]{1,0:T(8,128)(2,1)S(1)}, u32[]{:S(2)}) copy-start(bf16[16,512]{1,0:T(8,128)(2,1)S(1)} %squeeze.27) | copy-start | bytes 49156
  22.2 71.1 %copy-start.41 = (bf16[512,16]{1,0:T(8,128)(2,1)}, bf16[512,16]{1,0:T(8,128)(2,1)S(1)}, u32[]{:S(2)}) copy-start(bf16[512,16]{1,0:T(8,128)(2,1)S(1)} %squeeze.26) | copy-start | bytes 49156
  74.6 9.0 copy-start.23
  94.6 8.1 copy-start.67
  114.4 8.7 copy-start.30
  133.4 46.4 %copy-start.7 = (f32[1024,512]{1,0:T(8,128)}, f32[1024,512]{1,0:T(8,128)S(1)}, u32[]{:S(2)}) copy-start(f32[1024,512]{1,0:T(8,128)S(1)} %get-tuple-element.58) | copy-start | bytes 6291460
  133.9 21.8 %copy-start.81 = (bf16[2048,512]{1,0:T(8,128)(2,1)S(1)}, bf16[2048,512]{1,0:T(8,128)(2,1)}, u32[]{:S(2)}) copy-start(bf16[2048,512]{1,0:T(8,128)(2,1)} %param.35) | copy-start | bytes 6291460
  190.1 8.6 copy-start.31
  210.1 12.1 copy-start.22
  244.7 9.5 copy-start.24
  265.5 11.8 copy-start.21
  338.9 383.4 %copy-start.52 = (f32[1,1,16,512]{3,1,2,0:T(1,128)S(1)}, f32[1,1,16,512]{3,1,2,0:T(1,128)}, u32[]{:S(2)}) copy-start(f32[1,1,16,512]{3,1,2,0:T(1,128)} %copy.199) | copy-start | bytes 98308
  338.9 386.1 %copy-start.53 = (bf16[64,1536]{1,0:T(8,128)(2,1)S(1)}, bf16[64,1536]{1,0:T(8,128)(2,1)}, u32[]{:S(2)}) copy-start(bf16[64,1536]{1,0:T(8,128)(2,1)} %param.27) | copy-start | bytes 589828
  338.9 391.5 %copy-start.8 = (f32[1024,512]{1,0:T(8,128)S(1)}, f32[1024,512]{1,0:T(8,128)}, u32[]{:S(2)}) copy-start(f32[1024,512]{1,0:T(8,128)} %copy-done.7) | copy-start | bytes 6291460
  338.9 391.5 %copy-start.55 = (bf16[16,512]{1,0:T(8,128)(2,1)S(1)}, bf16[16,512]{1,0:T(8,128)(2,1)}, u32[]{:S(2)}) copy-start(bf16[16,512]{1,0:T(8,128)(2,1)} %copy-done.54) | copy-start | bytes 49156
  338.9 446.5 %all-gather.19.cloned.1.call-start = ((), (), s32[]{:S(2)}) async-start(), calls=%async_computation.5 | async-start | bytes 1081344 | tf_op jit(solution)/shard_map/all_gather | solution.py:259
  707.6 111.2 %all-gather.15.cloned.1.call-start = ((), (), s32[]{:S(2)}) async-start(), calls=%async_computation.3 | async-start | bytes 1081344 | tf_op jit(solution)/shard_map/all_gather | solution.py:257
  709.1 167.9 %all-gather.11.cloned.1.call-start = ((), (), s32[]{:S(2)}) async-start(), calls=%async_computation.1 | async-start | bytes 2162688 | tf_op jit(solution)/shard_map/all_gather | solution.py:263
  710.6 224.3 %all-gather.9.cloned.1.call-start = ((), (), s32[]{:S(2)}) async-start(), calls=%async_computation | async-start | bytes 2162688 | tf_op jit(solution)/shard_map/all_gather | solution.py:262
  712.2 283.9 %all-gather.17.cloned.1.call-start = ((), (), s32[]{:S(2)}) async-start(), calls=%async_computation.4 | async-start | bytes 3244032 | tf_op jit(solution)/shard_map/all_gather | solution.py:258
  713.8 343.5 %all-gather.13.cloned.1.call-start = ((), (), s32[]{:S(2)}) async-start(), calls=%async_computation.2 | async-start | bytes 3244032 | tf_op jit(solution)/shard_map/all_gather | solution.py:256
  715.4 406.2 %all-gather.23.cloned.1.call-start = ((), (), s32[]{:S(2)}) async-start(), calls=%async_computation.7 | async-start | bytes 4325376 | tf_op jit(solution)/shard_map/all_gather | solution.py:261
  717.0 468.6 %all-gather.21.cloned.1.call-start = ((), (), s32[]{:S(2)}) async-start(), calls=%async_computation.6 | async-start | bytes 4325376 | tf_op jit(solution)/shard_map/all_gather | solution.py:260
  718.7 591.5 %all-reduce.14.cloned.1.call-start = ((), (), s32[]{:S(2)}) async-start(), calls=%async_computation.8 | async-start | bytes 141312 | tf_op jit(solution)/shard_map/psum | solution.py:243
  1121.6 193.9 %copy-start.1 = (bf16[512,2048]{1,0:T(8,128)(2,1)S(1)}, bf16[512,2048]{1,0:T(8,128)(2,1)}, u32[]{:S(2)}) copy-start(bf16[512,2048]{1,0:T(8,128)(2,1)} %param.34) | copy-start | bytes 6291460
  (64 other events, 179.7 us)
Sparse Core Ops, SparseCore 0:
  339.0 367.2 all-reduce.15
  709.7 52.8 all-gather.18
  766.0 52.8 all-gather.14
  821.6 55.3 all-gather.10
  879.6 55.2 all-gather.8
  938.2 57.7 all-gather.16
  999.5 57.7 all-gather.12
  1060.7 60.8 all-gather.22
  1125.0 60.5 all-gather.20
  1192.2 117.9 all-reduce.13
where the time goes:
time: 1330 us; the launch traced here: 1320 us
  waiting for transfers between devices  863 us (65%)
  matrix products  187 us (14%)
  local copies, waits for them, and re-layouts  155 us (12%)
  other arithmetic  60 us (5%)
  blocking collectives  40.7 us (3%)
  between operations  16.4 us (1%)
    unnamed x11, waiting for transfers between devices  367 us
    psum x1, waiting for transfers between devices, on_device(): small = lax.psum((own_first, own_second, d_codes, own_task), 'dp')  120 us
    all_gather x1, waiting for transfers between devices, on_device(): lax.all_gather(shares[5], 'dp', axis=0, tiled=True)  59.8 us
    all_gather x1, waiting for transfers between devices, on_device(): lax.all_gather(shares[4], 'dp', axis=0, tiled=True)  59 us
    all_gather x1, waiting for transfers between devices, on_device(): lax.all_gather(shares[2], 'dp', axis=0, tiled=True)  58.4 us
    all_gather x1, waiting for transfers between devices, on_device(): lax.all_gather(shares[0], 'dp', axis=0, tiled=True)  56.7 us
    all_gather x1, waiting for transfers between devices, on_device(): lax.all_gather(shares[7], 'dp', axis=0, tiled=True)  55.7 us
    all_gather x1, waiting for transfers between devices, on_device(): lax.all_gather(shares[6], 'dp', axis=0, tiled=True)  55.2 us
  transfers between devices with their start and end apart: 10, of which 9 were waited for; matrix products, arithmetic and copies ran while one was open for 5% of the time, Pallas kernels for 0%

commit v1 on v0

--- a/solution.py
+++ b/solution.py
@@ -88,6 +88,40 @@
 
 def silu_back(values, grad_out):
     return jax.vjp(jax.nn.silu, values)[1](grad_out)[0]
+
+
+ORDER_A = ((1, 1), (2, 4), (4, 2), (8, 8), (16, 16))
+ORDER_B = ((1, 1), (2, 4), (8, 8), (16, 16), (4, 2))
+
+
+def all_sum(total, order):
+    devices = lax.axis_size("dp")
+    place = lax.axis_index("dp")
+
+    def swap(values, even_bit, odd_bit):
+        moves = [(i, i ^ (odd_bit if i % 2 else even_bit)) for i in range(devices)]
+        return lax.ppermute(values, "dp", moves)
+
+    def upper(even_bit, odd_bit):
+        return jnp.where(place % 2 == 1, (place // odd_bit) % 2, (place // even_bit) % 2)
+
+    for even_bit, odd_bit in order:
+        half = total.shape[0] // 2
+        side = upper(even_bit, odd_bit)
+        sent = lax.dynamic_slice_in_dim(total, (1 - side) * half, half)
+        kept = lax.dynamic_slice_in_dim(total, side * half, half)
+        total = kept + swap(sent, even_bit, odd_bit)
+    high = 32
+    while high < devices:
+        total = total + swap(total, high, high)
+        high *= 2
+    for even_bit, odd_bit in order[::-1]:
+        side = upper(even_bit, odd_bit)
+        other = swap(total, even_bit, odd_bit)
+        total = jnp.concatenate(
+            [jnp.where(side == 0, total, other), jnp.where(side == 0, other, total)]
+        )
+    return total
 
 
 def on_device(
@@ -229,9 +263,6 @@
     down_grads = jnp.stack([down_grad_one.reshape(-1), down_grad_two.reshape(-1)])
     up_grads = jnp.stack([up_grad_one.reshape(-1), up_grad_two.reshape(-1)])
     gain_grads = jnp.concatenate([gain_grad_one, gain_grad_two, gain_grad_three])
-    extra_down = jnp.dot(codes.T, down_grads, precision=highest).reshape(-1)
-    extra_up = jnp.dot(codes.T, up_grads, precision=highest).reshape(-1)
-    extra_gain = jnp.outer(code, gain_grads).reshape(-1)
     d_codes = jnp.dot(down_grads, down_f.T, precision=highest) + jnp.dot(
         up_grads, up_f.T, precision=highest
     )
@@ -240,50 +271,54 @@
     d_pre = silu_back(pre_act, jnp.dot(second_f, d_code, precision=highest))
     own_first = jnp.outer(embed, d_pre)
     own_task = jnp.outer(onehot, jnp.dot(first_f, d_pre, precision=highest))
-    small = lax.psum((own_first, own_second, d_codes, own_task), "dp")
-    shares = (
-        lax.psum_scatter(self_qkv_grad.reshape(-1), "dp", scatter_dimension=0, tiled=True),
-        lax.psum_scatter(self_out_grad.reshape(-1), "dp", scatter_dimension=0, tiled=True),
-        lax.psum_scatter(cross_qkv_grad.reshape(-1), "dp", scatter_dimension=0, tiled=True),
-        lax.psum_scatter(cross_out_grad.reshape(-1), "dp", scatter_dimension=0, tiled=True),
-        lax.psum_scatter(ffn_in_grad.reshape(-1), "dp", scatter_dimension=0, tiled=True),
-        lax.psum_scatter(ffn_out_grad.reshape(-1), "dp", scatter_dimension=0, tiled=True),
-        lax.psum_scatter(extra_down, "dp", scatter_dimension=0, tiled=True),
-        lax.psum_scatter(extra_up, "dp", scatter_dimension=0, tiled=True),
-        lax.psum_scatter(extra_gain, "dp", scatter_dimension=0, tiled=True),
-    )
-    whole = (
-        lax.all_gather(shares[0], "dp", axis=0, tiled=True),
-        lax.all_gather(shares[1], "dp", axis=0, tiled=True),
-        lax.all_gather(shares[2], "dp", axis=0, tiled=True),
-        lax.all_gather(shares[3], "dp", axis=0, tiled=True),
-        lax.all_gather(shares[4], "dp", axis=0, tiled=True),
-        lax.all_gather(shares[5], "dp", axis=0, tiled=True),
-        lax.all_gather(shares[6], "dp", axis=0, tiled=True),
-        lax.all_gather(shares[7], "dp", axis=0, tiled=True),
-        lax.all_gather(shares[8], "dp", axis=0, tiled=True),
-    )
-    hyper_down_grad = whole[6].reshape(emb_width, -1)
-    hyper_up_grad = whole[7].reshape(emb_width, -1)
-    hyper_gain_grad = whole[8].reshape(emb_width, -1)
-    hyper_first_grad, hyper_second_grad, position_grad, task_grad = small
+    spread = onehot[:, None, None]
+    small_parts = [
+        (spread * down_grads[None]).reshape(-1),
+        (spread * up_grads[None]).reshape(-1),
+        (onehot[:, None] * gain_grads[None]).reshape(-1),
+        own_first.reshape(-1),
+        own_second.reshape(-1),
+        d_codes.reshape(-1),
+        own_task.reshape(-1),
+    ]
+    small_flat = jnp.concatenate(small_parts)
+    unit = 8 * 32 * model_width
+    pad = (-small_flat.shape[0]) % unit
+    small_flat = jnp.concatenate([small_flat, jnp.zeros((pad,), jnp.float32)])
+    sum_out = all_sum(ffn_out_grad, ORDER_A)
+    sum_in = all_sum(ffn_in_grad, ORDER_B)
+    cross_rows = jnp.concatenate([cross_out_grad[None], cross_qkv_grad]).reshape(-1, model_width)
+    sum_cross = all_sum(cross_rows, ORDER_A).reshape(4, model_width, model_width)
+    self_rows = jnp.concatenate([self_out_grad[None], self_qkv_grad]).reshape(-1, model_width)
+    sum_self = all_sum(self_rows, ORDER_B).reshape(4, model_width, model_width)
+    sum_small = all_sum(small_flat.reshape(-1, model_width), ORDER_A).reshape(-1)
+    sums, at = [], 0
+    for part in small_parts:
+        sums.append(sum_small[at : at + part.shape[0]])
+        at += part.shape[0]
+    every_hidden = jax.nn.silu(jnp.dot(table, first_f, precision=highest))
+    every_code = jnp.dot(every_hidden, second_f, precision=highest)
+    every_codes = (every_code[:, None, :] + position_f[None]).reshape(-1, emb_width)
+    hyper_down_grad = jnp.dot(every_codes.T, sums[0].reshape(2 * ntask, -1), precision=highest)
+    hyper_up_grad = jnp.dot(every_codes.T, sums[1].reshape(2 * ntask, -1), precision=highest)
+    hyper_gain_grad = jnp.dot(every_code.T, sums[2].reshape(ntask, -1), precision=highest)
     return (
         output,
         input_grad,
         memory_grad.reshape(mem_shape),
-        task_grad,
-        position_grad,
-        hyper_first_grad,
-        hyper_second_grad,
+        sums[6].reshape(ntask, emb_width),
+        sums[5].reshape(2, emb_width),
+        sums[3].reshape(hyper_first.shape),
+        sums[4].reshape(hyper_second.shape),
         hyper_gain_grad,
         hyper_down_grad,
         hyper_up_grad,
-        whole[0].reshape(self_qkv.shape),
-        whole[1].reshape(self_out.shape),
-        whole[2].reshape(cross_qkv.shape),
-        whole[3].reshape(cross_out.shape),
-        whole[4].reshape(ffn_in.shape),
-        whole[5].reshape(ffn_out.shape),
+        sum_self[1:],
+        sum_self[0],
+        sum_cross[1:],
+        sum_cross[0],
+        sum_in,
+        sum_out,
     )
 
 

time: 1330 us -> 625 us (0.47)
  waiting for transfers between devices: 863 us -> 119 us
  starting transfers between devices: 0.42 us -> 71.5 us
  other arithmetic: 60 us -> 102 us
  blocking collectives: 40.7 us -> 0 us
  local copies, waits for them, and re-layouts: 155 us -> 121 us
    all_gather x8 -> x0, waiting for transfers between devices: 376 us -> none  [the longest x1 59.8 us: on_device(): lax.all_gather(shares[5], 'dp', axis=0, tiled=True)]
    unnamed x11 -> x0, waiting for transfers between devices: 367 us -> none
    psum x1 -> x0, waiting for transfers between devices: 120 us -> none  [on_device(): small = lax.psum((own_first, own_second, d_codes, own_task), 'dp')]
    ppermute x0 -> x50, waiting for transfers between devices: none -> 119 us  [swap(): return lax.ppermute(values, 'dp', moves)]
    ppermute x0 -> x50, starting transfers between devices: none -> 71.5 us  [swap(): return lax.ppermute(values, 'dp', moves)]
    all_gather x1 -> x0, blocking collectives: 40.7 us -> none  [on_device(): lax.all_gather(shares[8], 'dp', axis=0, tiled=True)]
    reshape x9 -> x7, local copies, waits for them, and re-layouts: 30.1 us -> 2.68 us  [the longest x1 1.69 us: on_device(): small_flat.reshape(-1, model_width)]
    unnamed x203 -> x275, local copies, waits for them, and re-layouts: 51.9 us -> 27.9 us
  transfers between devices with their start and end apart: 10 -> 50, of which waited for: 9 -> 22; matrix products, arithmetic and copies ran while one was open for 5% -> 38% of each run, Pallas kernels for 0% -> 0%
where the time goes in v1:
time: 625 us; the launch traced here: 615 us
  matrix products  197 us (32%)
  local copies, waits for them, and re-layouts  121 us (19%)
  waiting for transfers between devices  119 us (19%)
  other arithmetic  102 us (16%)
  starting transfers between devices  71.5 us (11%)
    ppermute x50, waiting for transfers between devices, swap(): return lax.ppermute(values, 'dp', moves)  119 us
    ppermute x50, starting transfers between devices, swap(): return lax.ppermute(values, 'dp', moves)  71.5 us
    another operation x14, local copies, waits for them, and re-layouts, split_heads(): return values.reshape(values.shape[0], values.shape[1], HEADS, HEAD_DIM)  42.2 us
    dot_general x9, matrix products, matmul(): return jnp.dot(left, right, preferred_element_type=jnp.float32)  33.2 us
    dot_general x2, matrix products, head_scores(): jnp.einsum('bqhd,bkhd->bhqk', head_q, head_k, preferred_element_type=jnp....  29.4 us
    unnamed x275, local copies, waits for them, and re-layouts  27.9 us
    convert_element_type x2, other arithmetic, attend_back(): grad_scores = (probs * (grad_probs - delta)).astype(jnp.bfloat16)  23.9 us
    dot_general x2, matrix products, attend_back(): jnp.einsum('bqhd,bkhd->bhqk', head_g, head_v, preferred_element_type=jnp....  22.8 us
  transfers between devices with their start and end apart: 50, of which 22 were waited for; matrix products, arithmetic and copies ran while one was open for 38% of the time, Pallas kernels for 0%

profile of v1, /device:TPU:0, one launch (start us, length us, event | category | flops | bytes accessed | tf_op | source)
XLA Modules:
  0.0 615.2 jit_solution(346561687866120832)
XLA Ops:
  29.3 3.9 reshape.416
  36.5 3.9 reshape.415
  52.5 10.2 %fusion.130 = (f32[2,8,512]{2,1,0:T(8,128)S(1)}, f32[2,8,512,512]{2,3,1,0:T(8,128)}) fusion(bf16[2,512,8,64]{1,3,2,0:T(8,128)(2,1)} %copy.67, bf16[2,512,8,64]{1,3,2,0:T(8,128)(2,1)} %copy.68, pred[2,512,512]{1,2,0:T(8,128)(4,1)S(1)} %compare_and_fusion), kind=kOutput, calls=%fused_computation.364 | convolution fusion | flops 549445632 | bytes 19431424 | tf_op jit(solution)/shard_map/bqhd,bkhd->bhqk/dot_general | solution.py:41
  62.7 8.4 %fusion = f32[2,8,512]{2,1,0:T(8,128)S(1)} fusion(f32[2,8,512,512]{2,3,1,0:T(8,128)} %get-tuple-element.111, f32[2,8,512]{2,1,0:T(8,128)S(1)} %get-tuple-element.110), kind=kLoop, calls=%fused_computation.11 | loop fusion | flops 8380416 | bytes 16842752 | tf_op jit(solution)/shard_map/reduce_sum | solution.py:53
  71.1 7.5 %fusion.43 = bf16[2,512,8,64]{1,3,2,0:T(8,128)(2,1)S(1)} fusion(bf16[2,512,8,64]{1,3,2,0:T(8,128)(2,1)S(1)} %copy-done.55, f32[2,8,512,512]{2,3,1,0:T(8,128)} %get-tuple-element.111, f32[2,8,512]{2,1,0:T(8,128)S(1)} %fusion, f32[2,8,512]{2,1,0:T(8,128)S(1)} %get-tuple-element.110), kind=kOutput, calls=%fused_computation.118 | convolution fusion | flops 549978112 | bytes 18939904 | tf_op jit(solution)/shard_map/bhqk,bkhd->bqhd/dot_general | solution.py:55
  90.7 19.3 %multiply_reduce_fusion.2 = (f32[2,8,512]{2,1,0:T(8,128)S(1)}, f32[2,8,512,512]{2,3,1,0:T(8,128)}) fusion(bf16[2,512,8,64]{1,3,2,0:T(8,128)(2,1)} %copy.74, bf16[2,512,8,64]{1,0,3,2:T(2,128)(2,1)S(1)} %copy-done.26), kind=kOutput, calls=%fused_computation.13 | convolution fusion | flops 545251328 | bytes 18907136 | tf_op jit(solution)/shard_map/bqhd,bkhd->bhqk/dot_general | solution.py:41
  110.0 8.7 %fusion.1 = f32[2,8,512]{2,1,0:T(8,128)S(1)} fusion(f32[2,8,512,512]{2,3,1,0:T(8,128)} %get-tuple-element.115, f32[2,8,512]{2,1,0:T(8,128)S(1)} %get-tuple-element.114), kind=kLoop, calls=%fused_computation.12 | loop fusion | flops 12574720 | bytes 16842752 | tf_op jit(solution)/shard_map/reduce_sum | solution.py:53
  118.7 7.7 %fusion.44 = bf16[2,512,8,64]{1,3,2,0:T(8,128)(2,1)S(1)} fusion(f32[2,8,512,512]{2,3,1,0:T(8,128)} %get-tuple-element.115, f32[2,8,512]{2,1,0:T(8,128)S(1)} %fusion.1, f32[2,8,512]{2,1,0:T(8,128)S(1)} %get-tuple-element.114, bf16[2,512,8,64]{1,0,3,2:T(2,128)(2,1)S(1)} %copy-done.67), kind=kOutput, calls=%fused_computation.119 | convolution fusion | flops 554172416 | bytes 18939904 | tf_op jit(solution)/shard_map/bhqk,bkhd->bqhd/dot_general | solution.py:55
  133.0 21.8 %multiply_convert_fusion.2 = (bf16[1024,2048]{1,0:T(8,128)(2,1)S(1)}, f32[1024,2048]{1,0:T(8,128)S(1)}, f32[1024,2048]{1,0:T(8,128)}) fusion(bf16[512,2048]{1,0:T(8,128)(2,1)S(1)} %copy-done, f32[1024,512]{1,0:T(8,128)S(1)} %copy-done.7, f32[512]{0:T(512)S(1)} %get-tuple-element.105, f32[1024]{0:T(1024)S(1)} %fusion.94), kind=kOutput, calls=%fused_computation.25 | convolution fusion | flops 2285371392 | bytes 25171968 | tf_op jit(solution)/shard_map/dot_general | solution.py:21
  158.5 7.5 %add_convert_fusion = bf16[1024,2048]{1,0:T(8,128)(2,1)S(1)} fusion(f32[1024,2048]{1,0:T(8,128)S(1)} %get-tuple-element.43, f32[1024,2048]{1,0:T(8,128)} %get-tuple-element.118, bf16[1024,512]{1,0:T(8,128)(2,1)S(1)} %fusion.23, bf16[2048,512]{1,0:T(8,128)(2,1)S(1)} %copy-done.120), kind=kOutput, calls=%fused_computation.24 | convolution fusion | flops 2176843776 | bytes 24117248 | tf_op jit(solution)/shard_map/dot_general | solution.py:31
  168.1 4.5 fusion.123
  176.3 6.6 %fusion.139 = f32[2048,512]{1,0:T(8,128)} fusion(bf16[1024,2048]{1,0:T(8,128)(2,1)} %copy-done.127, bf16[1024,512]{1,0:T(8,128)(2,1)S(1)} %copy-done.86), kind=kOutput, calls=%fused_computation.373 | convolution fusion | flops 2147483648 | bytes 9437184 | tf_op jit(solution)/shard_map/dot_general | solution.py:25
  186.2 5.0 multiply_reduce_fusion.3
  198.7 7.6 %fusion.34 = bf16[2,8,64,512]{3,2,1,0:T(8,128)(2,1)S(1)} fusion(bf16[2,512,8,64]{1,3,2,0:T(8,128)(2,1)S(1)} %copy.80, f32[2,8,512,512]{2,3,1,0:T(8,128)} %get-tuple-element.115, f32[2,8,512]{2,1,0:T(8,128)S(1)} %log_add_fusion.1), kind=kOutput, calls=%fused_computation.108 | convolution fusion | flops 549978112 | bytes 18907136 | tf_op jit(solution)/shard_map/bhqk,bqhd->bkhd/dot_general | solution.py:68
  206.3 11.8 %multiply_reduce_fusion.1 = (f32[2,8,512]{2,1,0:T(8,128)S(1)}, f32[2,8,512,512]{2,3,1,0:T(8,128)}) fusion(f32[2,8,512,512]{2,3,1,0:T(8,128)} %get-tuple-element.115, f32[2,8,512]{2,1,0:T(8,128)S(1)} %log_add_fusion.1, bf16[2,512,8,64]{1,3,2,0:T(8,128)(2,1)S(1)} %copy.80, bf16[2,512,8,64]{1,0,3,2:T(2,128)(2,1)S(1)} %copy-done.68), kind=kOutput, calls=%fused_computation.4 | convolution fusion | flops 553639936 | bytes 35717120 | tf_op jit(solution)/shard_map/bqhd,bkhd->bhqk/dot_general | solution.py:67
  218.1 12.1 %multiply_convert_fusion.1 = bf16[2,8,512,512]{2,3,1,0:T(8,128)(2,1)S(1)} fusion(f32[2,8,512,512]{2,3,1,0:T(8,128)} %get-tuple-element.123, f32[2,8,512,512]{2,3,1,0:T(8,128)} %get-tuple-element.115, f32[2,8,512]{2,1,0:T(8,128)S(1)} %get-tuple-element.122, f32[2,8,512]{2,1,0:T(8,128)S(1)} %log_add_fusion.1), kind=kLoop, calls=%fused_computation.3 | loop fusion | flops 20971520 | bytes 42008576 | tf_op jit(solution)/shard_map/convert_element_type | solution.py:72
  259.5 9.5 %fusion.40 = bf16[2,512,8,64]{1,3,2,0:T(8,128)(2,1)} fusion(bf16[2,512,8,64]{1,3,2,0:T(8,128)(2,1)S(1)} %copy.86, f32[2,8,512,512]{2,3,1,0:T(8,128)} %get-tuple-element.111, f32[2,8,512]{2,1,0:T(8,128)S(1)} %log_add_fusion), kind=kOutput, calls=%fused_computation.112 | convolution fusion | flops 545783808 | bytes 18907136 | tf_op jit(solution)/shard_map/bhqk,bqhd->bkhd/dot_general | solution.py:68
  269.0 11.1 %multiply_reduce_fusion = (f32[2,8,512]{2,1,0:T(8,128)S(1)}, f32[2,8,512,512]{2,3,1,0:T(8,128)}) fusion(f32[2,8,512,512]{2,3,1,0:T(8,128)} %get-tuple-element.111, f32[2,8,512]{2,1,0:T(8,128)S(1)} %log_add_fusion, bf16[2,512,8,64]{1,3,2,0:T(8,128)(2,1)S(1)} %copy.86, bf16[2,512,8,64]{1,3,2,0:T(8,128)(2,1)S(1)} %copy-done.56), kind=kOutput, calls=%fused_computation.1 | convolution fusion | flops 549445632 | bytes 35717120 | tf_op jit(solution)/shard_map/bqhd,bkhd->bhqk/dot_general | solution.py:67
  280.1 11.8 %multiply_convert_fusion = bf16[2,8,512,512]{2,3,1,0:T(8,128)(2,1)S(1)} fusion(f32[2,8,512,512]{2,3,1,0:T(8,128)} %get-tuple-element.126, f32[2,8,512,512]{2,3,1,0:T(8,128)} %get-tuple-element.111, f32[2,8,512]{2,1,0:T(8,128)S(1)} %get-tuple-element.125, f32[2,8,512]{2,1,0:T(8,128)S(1)} %log_add_fusion), kind=kLoop, calls=%fused_computation | loop fusion | flops 16777216 | bytes 42008576 | tf_op jit(solution)/shard_map/convert_element_type | solution.py:72
  333.7 4.2 convolution_bitcast_fusion
  385.6 6.2 %collective-permute-done.7 = f32[96,512]{1,0:T(8,128)S(1)} collective-permute-done((f32[96,512]{1,0:T(8,128)S(1)}, f32[96,512]{1,0:T(8,128)S(1)}, u32[]{:S(2)}, u32[]{:S(2)}) %collective-permute-start.7) | collective-permute-done | bytes 196640 | tf_op jit(solution)/shard_map/ppermute | solution.py:103
  426.8 16.4 %collective-permute-done.21 = f32[512,512]{1,0:T(8,128)} collective-permute-done((f32[512,512]{1,0:T(8,128)}, f32[512,512]{1,0:T(8,128)}, u32[]{:S(2)}, u32[]{:S(2)}) %collective-permute-start.21) | collective-permute-done | bytes 1048608 | tf_op jit(solution)/shard_map/ppermute | solution.py:103
  446.6 10.8 %collective-permute-done.11 = f32[512,512]{1,0:T(8,128)} collective-permute-done((f32[512,512]{1,0:T(8,128)}, f32[512,512]{1,0:T(8,128)}, u32[]{:S(2)}, u32[]{:S(2)}) %collective-permute-start.11) | collective-permute-done | bytes 1048608 | tf_op jit(solution)/shard_map/ppermute | solution.py:103
  466.1 10.0 %collective-permute-done.12 = f32[256,512]{1,0:T(8,128)S(1)} collective-permute-done((f32[256,512]{1,0:T(8,128)S(1)}, f32[256,512]{1,0:T(8,128)S(1)}, u32[]{:S(2)}, u32[]{:S(2)}) %collective-permute-start.12) | collective-permute-done | bytes 524320 | tf_op jit(solution)/shard_map/ppermute | solution.py:103
  488.6 5.1 collective-permute-done.13
  498.0 7.0 %collective-permute-done.24 = f32[64,512]{1,0:T(8,128)S(1)} collective-permute-done((f32[64,512]{1,0:T(8,128)S(1)}, f32[64,512]{1,0:T(8,128)S(1)}, u32[]{:S(2)}, u32[]{:S(2)}) %collective-permute-start.24) | collective-permute-done | bytes 131104 | tf_op jit(solution)/shard_map/ppermute | solution.py:103
  519.7 9.2 %collective-permute-done.26 = f32[128,512]{1,0:T(8,128)S(1)} collective-permute-done((f32[128,512]{1,0:T(8,128)S(1)}, f32[128,512]{1,0:T(8,128)S(1)}, u32[]{:S(2)}, u32[]{:S(2)}) %collective-permute-start.26) | collective-permute-done | bytes 262176 | tf_op jit(solution)/shard_map/ppermute | solution.py:103
  531.4 7.9 %collective-permute-done.27 = f32[256,512]{1,0:T(8,128)S(1)} collective-permute-done((f32[256,512]{1,0:T(8,128)S(1)}, f32[256,512]{1,0:T(8,128)S(1)}, u32[]{:S(2)}, u32[]{:S(2)}) %collective-permute-start.27) | collective-permute-done | bytes 524320 | tf_op jit(solution)/shard_map/ppermute | solution.py:103
  539.5 9.7 %collective-permute-start.28 = (f32[512,512]{1,0:T(8,128)S(1)}, f32[512,512]{1,0:T(8,128)S(1)}, u32[]{:S(2)}, u32[]{:S(2)}) collective-permute-start(f32[512,512]{1,0:T(8,128)S(1)} %pad_maximum_fusion.12), channel_id=1, source_target_pairs={{0,2},{1,5},{2,0},{3,7},{4,6},{5,1},{6,4},{7,3},{8,10},{9,13},{10,... | collective-permute-start | bytes 3145736 | tf_op jit(solution)/shard_map/ppermute | solution.py:103
  553.0 9.0 %collective-permute-done.28 = f32[512,512]{1,0:T(8,128)S(1)} collective-permute-done((f32[512,512]{1,0:T(8,128)S(1)}, f32[512,512]{1,0:T(8,128)S(1)}, u32[]{:S(2)}, u32[]{:S(2)}) %collective-permute-start.28) | collective-permute-done | bytes 1048608 | tf_op jit(solution)/shard_map/ppermute | solution.py:103
  563.9 9.3 %collective-permute-done.18 = f32[512,512]{1,0:T(8,128)S(1)} collective-permute-done((f32[512,512]{1,0:T(8,128)S(1)}, f32[512,512]{1,0:T(8,128)S(1)}, u32[]{:S(2)}, u32[]{:S(2)}) %collective-permute-start.18) | collective-permute-done | bytes 1048608 | tf_op jit(solution)/shard_map/ppermute | solution.py:103
  590.5 5.2 collective-permute-done.48
  (601 shorter events, 322.3 us)
Async XLA Ops:
  175.8 217.6 %collective-permute-start.30 = (f32[256,2048]{1,0:T(8,128)}, f32[256,2048]{1,0:T(8,128)}, u32[]{:S(2)}, u32[]{:S(2)}) collective-permute-start(f32[256,2048]{1,0:T(8,128)} %constant_dynamic-slice_fusion.9), channel_id=1, source_target_pairs={{0,1},{1,0},{2,3},{3,2},{4,5},{5,4},{6,7},{7,6},{8,9},{9,8},{10,11... | collective-permute-start | bytes 6291464 | tf_op jit(solution)/shard_map/ppermute | solution.py:103
  186.1 211.8 %collective-permute-start.40 = (f32[1024,512]{1,0:T(8,128)}, f32[1024,512]{1,0:T(8,128)}, u32[]{:S(2)}, u32[]{:S(2)}) collective-permute-start(f32[1024,512]{1,0:T(8,128)} %constant_dynamic-slice_fusion.4), channel_id=1, source_target_pairs={{0,1},{1,0},{2,3},{3,2},{4,5},{5,4},{6,7},{7,6},{8,9},{9,8},{10,11... | collective-permute-start | bytes 6291464 | tf_op jit(solution)/shard_map/ppermute | solution.py:103
  242.8 159.9 %collective-permute-start.20 = (f32[1024,512]{1,0:T(8,128)}, f32[1024,512]{1,0:T(8,128)}, u32[]{:S(2)}, u32[]{:S(2)}) collective-permute-start(f32[1024,512]{1,0:T(8,128)} %constant_dynamic-slice_fusion.14), channel_id=1, source_target_pairs={{0,1},{1,0},{2,3},{3,2},{4,5},{5,4},{6,7},{7,6},{8,9},{9,8},{10,11... | collective-permute-start | bytes 6291464 | tf_op jit(solution)/shard_map/ppermute | solution.py:103
  341.7 66.4 %collective-permute-start.10 = (f32[1024,512]{1,0:T(8,128)}, f32[1024,512]{1,0:T(8,128)}, u32[]{:S(2)}, u32[]{:S(2)}) collective-permute-start(f32[1024,512]{1,0:T(8,128)} %constant_dynamic-slice_fusion.19), channel_id=1, source_target_pairs={{0,1},{1,0},{2,3},{3,2},{4,5},{5,4},{6,7},{7,6},{8,9},{9,8},{10,11... | collective-permute-start | bytes 6291464 | tf_op jit(solution)/shard_map/ppermute | solution.py:103
  397.3 21.6 %collective-permute-start.31 = (f32[128,2048]{1,0:T(8,128)}, f32[128,2048]{1,0:T(8,128)}, u32[]{:S(2)}, u32[]{:S(2)}) collective-permute-start(f32[128,2048]{1,0:T(8,128)} %constant_dynamic-slice_fusion.8), channel_id=1, source_target_pairs={{0,2},{1,5},{2,0},{3,7},{4,6},{5,1},{6,4},{7,3},{8,10},{9,13},{10,... | collective-permute-start | bytes 3145736 | tf_op jit(solution)/shard_map/ppermute | solution.py:103
  401.0 22.7 %collective-permute-start.41 = (f32[512,512]{1,0:T(8,128)}, f32[512,512]{1,0:T(8,128)}, u32[]{:S(2)}, u32[]{:S(2)}) collective-permute-start(f32[512,512]{1,0:T(8,128)} %constant_dynamic-slice_fusion.3), channel_id=1, source_target_pairs={{0,2},{1,5},{2,0},{3,7},{4,6},{5,1},{6,4},{7,3},{8,10},{9,13},{10,... | collective-permute-start | bytes 3145736 | tf_op jit(solution)/shard_map/ppermute | solution.py:103
  406.6 36.5 %collective-permute-start.21 = (f32[512,512]{1,0:T(8,128)}, f32[512,512]{1,0:T(8,128)}, u32[]{:S(2)}, u32[]{:S(2)}) collective-permute-start(f32[512,512]{1,0:T(8,128)} %constant_dynamic-slice_fusion.13), channel_id=1, source_target_pairs={{0,2},{1,5},{2,0},{3,7},{4,6},{5,1},{6,4},{7,3},{8,10},{9,13},{10,... | collective-permute-start | bytes 3145736 | tf_op jit(solution)/shard_map/ppermute | solution.py:103
  411.6 45.8 %collective-permute-start.11 = (f32[512,512]{1,0:T(8,128)}, f32[512,512]{1,0:T(8,128)}, u32[]{:S(2)}, u32[]{:S(2)}) collective-permute-start(f32[512,512]{1,0:T(8,128)} %constant_dynamic-slice_fusion.18), channel_id=1, source_target_pairs={{0,2},{1,5},{2,0},{3,7},{4,6},{5,1},{6,4},{7,3},{8,10},{9,13},{10,... | collective-permute-start | bytes 3145736 | tf_op jit(solution)/shard_map/ppermute | solution.py:103
  420.8 40.2 %collective-permute-start.32 = (f32[64,2048]{1,0:T(8,128)S(1)}, f32[64,2048]{1,0:T(8,128)S(1)}, u32[]{:S(2)}, u32[]{:S(2)}) collective-permute-start(f32[64,2048]{1,0:T(8,128)S(1)} %constant_dynamic-slice_fusion.7), channel_id=1, source_target_pairs={{0,8},{1,9},{2,10},{3,11},{4,12},{5,13},{6,14},{7,15},{8,0},{9,1},... | collective-permute-start | bytes 1572872 | tf_op jit(solution)/shard_map/ppermute | solution.py:103
  425.2 38.5 %collective-permute-start.42 = (f32[256,512]{1,0:T(8,128)S(1)}, f32[256,512]{1,0:T(8,128)S(1)}, u32[]{:S(2)}, u32[]{:S(2)}) collective-permute-start(f32[256,512]{1,0:T(8,128)S(1)} %constant_dynamic-slice_fusion.2), channel_id=1, source_target_pairs={{0,4},{1,3},{2,6},{3,1},{4,0},{5,7},{6,2},{7,5},{8,12},{9,11},{10,... | collective-permute-start | bytes 1572872 | tf_op jit(solution)/shard_map/ppermute | solution.py:103
  444.7 19.2 %collective-permute-start.22 = (f32[256,512]{1,0:T(8,128)S(1)}, f32[256,512]{1,0:T(8,128)S(1)}, u32[]{:S(2)}, u32[]{:S(2)}) collective-permute-start(f32[256,512]{1,0:T(8,128)S(1)} %constant_dynamic-slice_fusion.12), channel_id=1, source_target_pairs={{0,4},{1,3},{2,6},{3,1},{4,0},{5,7},{6,2},{7,5},{8,12},{9,11},{10,... | collective-permute-start | bytes 1572872 | tf_op jit(solution)/shard_map/ppermute | solution.py:103
  458.9 17.2 %collective-permute-start.12 = (f32[256,512]{1,0:T(8,128)S(1)}, f32[256,512]{1,0:T(8,128)S(1)}, u32[]{:S(2)}, u32[]{:S(2)}) collective-permute-start(f32[256,512]{1,0:T(8,128)S(1)} %constant_dynamic-slice_fusion.17), channel_id=1, source_target_pairs={{0,8},{1,9},{2,10},{3,11},{4,12},{5,13},{6,14},{7,15},{8,0},{9,1},... | collective-permute-start | bytes 1572872 | tf_op jit(solution)/shard_map/ppermute | solution.py:103
  461.1 15.7 %collective-permute-start.33 = (f32[32,2048]{1,0:T(8,128)S(1)}, f32[32,2048]{1,0:T(8,128)S(1)}, u32[]{:S(2)}, u32[]{:S(2)}) collective-permute-start(f32[32,2048]{1,0:T(8,128)S(1)} %constant_dynamic-slice_fusion.6), channel_id=1, source_target_pairs={{0,16},{1,17},{2,18},{3,19},{4,20},{5,21},{6,22},{7,23},{8,24},{9,... | collective-permute-start | bytes 786440 | tf_op jit(solution)/shard_map/ppermute | solution.py:103
  463.8 16.6 %collective-permute-start.43 = (f32[128,512]{1,0:T(8,128)S(1)}, f32[128,512]{1,0:T(8,128)S(1)}, u32[]{:S(2)}, u32[]{:S(2)}) collective-permute-start(f32[128,512]{1,0:T(8,128)S(1)} %constant_dynamic-slice_fusion.1), channel_id=1, source_target_pairs={{0,8},{1,9},{2,10},{3,11},{4,12},{5,13},{6,14},{7,15},{8,0},{9,1},... | collective-permute-start | bytes 786440 | tf_op jit(solution)/shard_map/ppermute | solution.py:103
  464.0 23.3 %collective-permute-start.23 = (f32[128,512]{1,0:T(8,128)S(1)}, f32[128,512]{1,0:T(8,128)S(1)}, u32[]{:S(2)}, u32[]{:S(2)}) collective-permute-start(f32[128,512]{1,0:T(8,128)S(1)} %constant_dynamic-slice_fusion.11), channel_id=1, source_target_pairs={{0,8},{1,9},{2,10},{3,11},{4,12},{5,13},{6,14},{7,15},{8,0},{9,1},... | collective-permute-start | bytes 786440 | tf_op jit(solution)/shard_map/ppermute | solution.py:103
  476.2 17.5 %collective-permute-start.13 = (f32[128,512]{1,0:T(8,128)S(1)}, f32[128,512]{1,0:T(8,128)S(1)}, u32[]{:S(2)}, u32[]{:S(2)}) collective-permute-start(f32[128,512]{1,0:T(8,128)S(1)} %constant_dynamic-slice_fusion.16), channel_id=1, source_target_pairs={{0,16},{1,17},{2,18},{3,19},{4,20},{5,21},{6,22},{7,23},{8,24},{9,... | collective-permute-start | bytes 786440 | tf_op jit(solution)/shard_map/ppermute | solution.py:103
  476.9 18.5 %collective-permute-start.34 = (f32[16,2048]{1,0:T(8,128)S(1)}, f32[16,2048]{1,0:T(8,128)S(1)}, u32[]{:S(2)}, u32[]{:S(2)}) collective-permute-start(f32[16,2048]{1,0:T(8,128)S(1)} %constant_dynamic-slice_fusion.5), channel_id=1, source_target_pairs={{0,4},{1,3},{2,6},{3,1},{4,0},{5,7},{6,2},{7,5},{8,12},{9,11},{10,... | collective-permute-start | bytes 393224 | tf_op jit(solution)/shard_map/ppermute | solution.py:103
  480.5 17.4 %collective-permute-start.44 = (f32[64,512]{1,0:T(8,128)S(1)}, f32[64,512]{1,0:T(8,128)S(1)}, u32[]{:S(2)}, u32[]{:S(2)}) collective-permute-start(f32[64,512]{1,0:T(8,128)S(1)} %constant_dynamic-slice_fusion), channel_id=1, source_target_pairs={{0,16},{1,17},{2,18},{3,19},{4,20},{5,21},{6,22},{7,23},{8,24},{9,... | collective-permute-start | bytes 393224 | tf_op jit(solution)/shard_map/ppermute | solution.py:103
  487.4 17.7 %collective-permute-start.24 = (f32[64,512]{1,0:T(8,128)S(1)}, f32[64,512]{1,0:T(8,128)S(1)}, u32[]{:S(2)}, u32[]{:S(2)}) collective-permute-start(f32[64,512]{1,0:T(8,128)S(1)} %constant_dynamic-slice_fusion.10), channel_id=1, source_target_pairs={{0,16},{1,17},{2,18},{3,19},{4,20},{5,21},{6,22},{7,23},{8,24},{9,... | collective-permute-start | bytes 393224 | tf_op jit(solution)/shard_map/ppermute | solution.py:103
  509.8 21.0 %collective-permute-start.46 = (f32[128,512]{1,0:T(8,128)S(1)}, f32[128,512]{1,0:T(8,128)S(1)}, u32[]{:S(2)}, u32[]{:S(2)}) collective-permute-start(f32[128,512]{1,0:T(8,128)S(1)} %pad_maximum_fusion.24), channel_id=1, source_target_pairs={{0,8},{1,9},{2,10},{3,11},{4,12},{5,13},{6,14},{7,15},{8,0},{9,1},... | collective-permute-start | bytes 786440 | tf_op jit(solution)/shard_map/ppermute | solution.py:103
  512.0 16.9 %collective-permute-start.26 = (f32[128,512]{1,0:T(8,128)S(1)}, f32[128,512]{1,0:T(8,128)S(1)}, u32[]{:S(2)}, u32[]{:S(2)}) collective-permute-start(f32[128,512]{1,0:T(8,128)S(1)} %pad_maximum_fusion.22), channel_id=1, source_target_pairs={{0,8},{1,9},{2,10},{3,11},{4,12},{5,13},{6,14},{7,15},{8,0},{9,1},... | collective-permute-start | bytes 786440 | tf_op jit(solution)/shard_map/ppermute | solution.py:103
  512.2 18.4 %collective-permute-start.16 = (f32[128,512]{1,0:T(8,128)S(1)}, f32[128,512]{1,0:T(8,128)S(1)}, u32[]{:S(2)}, u32[]{:S(2)}) collective-permute-start(f32[128,512]{1,0:T(8,128)S(1)} %pad_maximum_fusion.21), channel_id=1, source_target_pairs={{0,16},{1,17},{2,18},{3,19},{4,20},{5,21},{6,22},{7,23},{8,24},{9,... | collective-permute-start | bytes 786440 | tf_op jit(solution)/shard_map/ppermute | solution.py:103
  516.6 33.0 %collective-permute-start.37 = (f32[64,2048]{1,0:T(8,128)S(1)}, f32[64,2048]{1,0:T(8,128)S(1)}, u32[]{:S(2)}, u32[]{:S(2)}) collective-permute-start(f32[64,2048]{1,0:T(8,128)S(1)} %pad_maximum_fusion.18), channel_id=1, source_target_pairs={{0,8},{1,9},{2,10},{3,11},{4,12},{5,13},{6,14},{7,15},{8,0},{9,1},... | collective-permute-start | bytes 1572872 | tf_op jit(solution)/shard_map/ppermute | solution.py:103
  530.7 18.5 %collective-permute-start.17 = (f32[256,512]{1,0:T(8,128)S(1)}, f32[256,512]{1,0:T(8,128)S(1)}, u32[]{:S(2)}, u32[]{:S(2)}) collective-permute-start(f32[256,512]{1,0:T(8,128)S(1)} %pad_maximum_fusion.16), channel_id=1, source_target_pairs={{0,8},{1,9},{2,10},{3,11},{4,12},{5,13},{6,14},{7,15},{8,0},{9,1},... | collective-permute-start | bytes 1572872 | tf_op jit(solution)/shard_map/ppermute | solution.py:103
  530.9 22.0 %collective-permute-start.47 = (f32[256,512]{1,0:T(8,128)S(1)}, f32[256,512]{1,0:T(8,128)S(1)}, u32[]{:S(2)}, u32[]{:S(2)}) collective-permute-start(f32[256,512]{1,0:T(8,128)S(1)} %pad_maximum_fusion.19), channel_id=1, source_target_pairs={{0,4},{1,3},{2,6},{3,1},{4,0},{5,7},{6,2},{7,5},{8,12},{9,11},{10,... | collective-permute-start | bytes 1572872 | tf_op jit(solution)/shard_map/ppermute | solution.py:103
  539.5 22.5 %collective-permute-start.28 = (f32[512,512]{1,0:T(8,128)S(1)}, f32[512,512]{1,0:T(8,128)S(1)}, u32[]{:S(2)}, u32[]{:S(2)}) collective-permute-start(f32[512,512]{1,0:T(8,128)S(1)} %pad_maximum_fusion.12), channel_id=1, source_target_pairs={{0,2},{1,5},{2,0},{3,7},{4,6},{5,1},{6,4},{7,3},{8,10},{9,13},{10,... | collective-permute-start | bytes 3145736 | tf_op jit(solution)/shard_map/ppermute | solution.py:103
  549.4 23.8 %collective-permute-start.18 = (f32[512,512]{1,0:T(8,128)S(1)}, f32[512,512]{1,0:T(8,128)S(1)}, u32[]{:S(2)}, u32[]{:S(2)}) collective-permute-start(f32[512,512]{1,0:T(8,128)S(1)} %pad_maximum_fusion.11), channel_id=1, source_target_pairs={{0,2},{1,5},{2,0},{3,7},{4,6},{5,1},{6,4},{7,3},{8,10},{9,13},{10,... | collective-permute-start | bytes 3145736 | tf_op jit(solution)/shard_map/ppermute | solution.py:103
  550.9 36.6 %collective-permute-start.38 = (f32[128,2048]{1,0:T(8,128)}, f32[128,2048]{1,0:T(8,128)}, u32[]{:S(2)}, u32[]{:S(2)}) collective-permute-start(f32[128,2048]{1,0:T(8,128)} %pad_maximum_fusion.13), channel_id=1, source_target_pairs={{0,2},{1,5},{2,0},{3,7},{4,6},{5,1},{6,4},{7,3},{8,10},{9,13},{10,... | collective-permute-start | bytes 3145736 | tf_op jit(solution)/shard_map/ppermute | solution.py:103
  563.9 32.4 %collective-permute-start.29 = (f32[1024,512]{1,0:T(8,128)}, f32[1024,512]{1,0:T(8,128)}, u32[]{:S(2)}, u32[]{:S(2)}) collective-permute-start(f32[1024,512]{1,0:T(8,128)} %pad_maximum_fusion.7), channel_id=1, source_target_pairs={{0,1},{1,0},{2,3},{3,2},{4,5},{5,4},{6,7},{7,6},{8,9},{9,8},{10,11... | collective-permute-start | bytes 6291464 | tf_op jit(solution)/shard_map/ppermute | solution.py:103
  575.5 25.0 %collective-permute-start.19 = (f32[1024,512]{1,0:T(8,128)}, f32[1024,512]{1,0:T(8,128)}, u32[]{:S(2)}, u32[]{:S(2)}) collective-permute-start(f32[1024,512]{1,0:T(8,128)} %pad_maximum_fusion.6), channel_id=1, source_target_pairs={{0,1},{1,0},{2,3},{3,2},{4,5},{5,4},{6,7},{7,6},{8,9},{9,8},{10,11... | collective-permute-start | bytes 6291464 | tf_op jit(solution)/shard_map/ppermute | solution.py:103
  576.6 19.2 %collective-permute-start.48 = (f32[512,512]{1,0:T(8,128)}, f32[512,512]{1,0:T(8,128)S(1)}, u32[]{:S(2)}, u32[]{:S(2)}) collective-permute-start(f32[512,512]{1,0:T(8,128)} %pad_maximum_fusion.14), channel_id=1, source_target_pairs={{0,2},{1,5},{2,0},{3,7},{4,6},{5,1},{6,4},{7,3},{8,10},{9,13},{10,... | collective-permute-start | bytes 3145736 | tf_op jit(solution)/shard_map/ppermute | solution.py:103
  589.2 19.4 %collective-permute-start.39 = (f32[256,2048]{1,0:T(8,128)S(1)}, f32[256,2048]{1,0:T(8,128)S(1)}, u32[]{:S(2)}, u32[]{:S(2)}) collective-permute-start(f32[256,2048]{1,0:T(8,128)S(1)} %pad_maximum_fusion.8), channel_id=1, source_target_pairs={{0,1},{1,0},{2,3},{3,2},{4,5},{5,4},{6,7},{7,6},{8,9},{9,8},{10,11... | collective-permute-start | bytes 6291464 | tf_op jit(solution)/shard_map/ppermute | solution.py:103
  (146 other events, 1244.0 us)
